TPU v7x, 32 devices: a whole 2x2x4 slice. The times are simulated.
32 devices in a mesh: grp: 2 (over y), tm: 4 (over z), freq: 4 (over x, core).
Axes of the slice: x: 2, y: 2, z: 4, core: 2. Of those that a mesh axis runs over, the one named last changes fastest.
Arguments:
- visibilities: bfloat16 [2, 132, 64, 1536], P(None, 'grp', 'tm', 'freq'), parts along dimension 1, may hold values from -6 to 6
- class_ids: int32 [132], P('grp'), parts along dimension 0, may hold values from 0 to 3, as said below
- class_counts: int32 [8], P('grp'), parts along dimension 0, may hold values from 1 to 32, as said below
- tap_windows: int32 [8], P('grp'), parts along dimension 0, may hold values from 1 to 4, as said below
- fringe_taps: float32 [2, 8, 9], P(None, 'grp'), parts along dimension 1, may hold values from -2.4 to 2.4
- flag_mask: int32 [64, 1536], P('freq'), may hold values 0 or 1
- filter_panels: bfloat16 [8, 1536, 1536], P(('grp', 'tm'), 'freq'), parts along dimension 0
Outputs:
- cleaned: bfloat16 [2, 8, 32, 64, 1536], P(None, ('grp', 'tm'), None, 'freq'), parts along dimension 1
There are 2 independent parts, one for each index of `grp`. A program takes and returns all parts, laid end to end along the dimension named above; an argument that names none is the same for every part. Nothing has to cross between parts.
Inputs may be any that keep to these rules, and one draw needn't show every extreme that they name: Baselines are listed grouped by class in increasing order of class; class_ids[b] is the class of baseline b. class_counts[c] is the number of baselines whose class is c; some class has exactly 32 baselines. `tap_windows`: some class has a window of exactly 4.
All inputs are finite; a program needn't handle non-finite values. No bound on the sum of `flag_mask` on one device may be relied on, other than what follows from the above.
Results may differ from a plain program's by a relative error of at most 0.0049.
Values may be sent and summed in bfloat16 or wider, within the bound.
A program may use at most 128 MiB of HBM per device.

v0:
```python
import jax
import jax.numpy as jnp
from jax import lax
from jax.sharding import PartitionSpec as P

SLOTS = 32
REACH = 4


def extended(cells, sides, width):
    for axis, dim in sides:
        count = lax.axis_size(axis)
        ends = count - 1
        head = lax.slice_in_dim(cells, 0, width, axis=dim)
        tail = lax.slice_in_dim(cells, cells.shape[dim] - width, cells.shape[dim], axis=dim)
        cells = jnp.concatenate(
            [
                lax.ppermute(tail, axis, [(i, (i + 1) % count) for i in range(ends)]),
                cells,
                lax.ppermute(head, axis, [((i + 1) % count, i) for i in range(ends)]),
            ],
            axis=dim,
        )
    return cells


def masked_taps(fringe_taps, tap_windows):
    offsets = jnp.abs(jnp.arange(2 * REACH + 1, dtype=jnp.int32) - REACH)
    keep = (offsets[None, :] <= tap_windows[:, None]).astype(jnp.float32)
    return fringe_taps * keep[None, :, :]


def convolve(padded, row_taps, length):
    real_part = jnp.zeros(padded.shape[1:2] + (length,) + padded.shape[3:], jnp.float32)
    imag_part = jnp.zeros_like(real_part)
    for offset in range(2 * REACH + 1):
        shifted = lax.slice_in_dim(padded, 2 * REACH - offset, 2 * REACH - offset + length, axis=2)
        tap_real = row_taps[0, :, offset][:, None, None]
        tap_imag = row_taps[1, :, offset][:, None, None]
        real_part = real_part + tap_real * shifted[0] - tap_imag * shifted[1]
        imag_part = imag_part + tap_real * shifted[1] + tap_imag * shifted[0]
    return jnp.stack([real_part, imag_part]).astype(jnp.bfloat16)


def to_slots(per_baseline, class_counts):
    class_starts = jnp.cumsum(class_counts) - class_counts
    slot_positions = jnp.arange(SLOTS, dtype=jnp.int32)
    input_visibility = jnp.clip(
        class_starts[:, None] + slot_positions[None, :], 0, per_baseline.shape[1] - 1
    )
    live_slot = slot_positions[None, :] < class_counts[:, None]
    gathered = jnp.take(per_baseline, input_visibility.reshape(-1), axis=1)
    gathered = gathered.reshape(per_baseline.shape[:1] + live_slot.shape + per_baseline.shape[2:])
    return jnp.where(live_slot[None, :, :, None, None], gathered, jnp.zeros((), per_baseline.dtype))


def shards(
    visibilities, class_ids, class_counts, tap_windows, fringe_taps, flag_mask, filter_panels
):
    taps_kept = masked_taps(fringe_taps, tap_windows)
    padded = extended(visibilities, (("tm", 2),), REACH)
    class_iota = jnp.arange(taps_kept.shape[1], dtype=jnp.int32)
    one_hot = (class_ids[:, None] == class_iota[None, :]).astype(jnp.float32)
    row_taps = jnp.einsum("bc,rck->rbk", one_hot, taps_kept, precision=lax.Precision.HIGHEST)
    filtered = convolve(padded, row_taps, visibilities.shape[2])
    slotted = to_slots(filtered, class_counts)
    local_block = lax.all_to_all(
        lax.all_to_all(slotted, "tm", split_axis=1, concat_axis=3, tiled=True),
        "freq",
        split_axis=3,
        concat_axis=4,
        tiled=True,
    )
    flag_gate = flag_mask.astype(jnp.bfloat16)
    weighted = local_block * flag_gate
    dayenu_fit = jnp.einsum(
        "rcstj,cij->rcsti",
        weighted,
        lax.all_gather(filter_panels, "freq", axis=1, tiled=True),
        preferred_element_type=jnp.float32,
    )
    return (local_block.astype(jnp.float32) - dayenu_fit).astype(jnp.bfloat16)


def solution(mesh):
    return jax.shard_map(
        shards,
        mesh=mesh,
        in_specs=(
            P(None, "grp", "tm", "freq"),
            P("grp"),
            P("grp"),
            P("grp"),
            P(None, "grp", None),
            P("freq", None),
            P(("grp", "tm"), "freq", None),
        ),
        out_specs=P(None, ("grp", "tm"), None, "freq", None),
        check_vma=False,
    )
```

profile of v0, /device:TPU:0, one launch (start us, length us, event | category | flops | bytes accessed | tf_op | source)
XLA Modules:
  0.0 189.7 jit_solution(7154030668723489211)
XLA Ops:
  6.5 0.0 copy-start
  6.5 0.0 copy-start.4
  6.5 0.0 copy-start.5
  6.5 0.0 copy-start.2
  6.5 0.0 copy-start.3
  6.5 1.8 fusion.57
  8.4 1.3 collective-permute-start
  9.7 5.6 %collective-permute-start.1 = (bf16[2,66,4,384]{3,2,1,0:T(4,128)(2,1)S(1)}, bf16[2,66,4,384]{3,2,1,0:T(4,128)(2,1)S(1)}, u32[]{:S(2)}, u32[]{:S(2)}) collective-permute-start(bf16[2,66,4,384]{3,2,1,0:T(4,128)(2,1)S(1)} %get-tuple-element.7), channel_id=1, source_target_pairs={{0,4},{4,8},{8,12},{1,5},{5,9},{9,13},{2,6},{6,10},{10,14},{3,7},{... | collective-permute-start | bytes 1216520 | tf_op jit(solution)/shard_map/ppermute | solution.py:18
  15.3 0.0 copy-done.4
  15.3 0.2 reduce-window.9
  15.5 0.1 add_clamp_fusion
  15.5 0.1 iota_compare_fusion.1
  15.6 0.1 min.12
  15.7 0.0 copy-done.5
  15.7 0.1 compare_convert_fusion
  15.8 0.0 copy-done.2
  15.8 0.0 copy-done.3
  15.8 0.2 convolution_bitcast_fusion
  16.0 0.0 copy-done
  16.0 0.2 constant_dynamic-update-slice_fusion.1
  16.2 6.5 %collective-permute-done = bf16[2,66,4,384]{3,2,1,0:T(4,128)(2,1)S(1)} collective-permute-done((bf16[2,66,4,384]{3,2,1,0:T(4,128)(2,1)S(1)}, bf16[2,66,4,384]{3,2,1,0:T(4,128)(2,1)S(1)}, u32[]{:S(2)}, u32[]{:S(2)}) %collective-permute-start) | collective-permute-done | bytes 405536 | tf_op jit(solution)/shard_map/ppermute | solution.py:20
  22.7 0.3 constant_dynamic-update-slice_fusion
  23.0 0.9 collective-permute-done.1
  23.9 5.1 %fusion.43 = bf16[1,66,16,384]{3,2,1,0:T(8,128)(2,1)S(1)} fusion(f32[66]{0:T(128)S(1)} %get-tuple-element.10, f32[66]{0:T(128)S(1)} %get-tuple-element.11, f32[66]{0:T(128)S(1)} %get-tuple-element.12, f32[66]{0:T(128)S(1)} %get-tuple-element.13, f32[66]{0:T(128)S(1)} %get-tuple-element.14, f32[66]{0:T(128)S(1)} %get-tuple-element.15, ...), kind=kLoop, calls=%fused_computation.94 | loop fusion | flops 31629312 | bytes 10957824 | tf_op jit(solution)/shard_map/convert.1
  29.0 5.2 %fusion.42 = bf16[1,66,16,384]{3,2,1,0:T(8,128)(2,1)S(1)} fusion(f32[66]{0:T(128)S(1)} %get-tuple-element.10, f32[66]{0:T(128)S(1)} %get-tuple-element.11, f32[66]{0:T(128)S(1)} %get-tuple-element.12, f32[66]{0:T(128)S(1)} %get-tuple-element.13, f32[66]{0:T(128)S(1)} %get-tuple-element.14, f32[66]{0:T(128)S(1)} %get-tuple-element.15, ...), kind=kLoop, calls=%fused_computation.93 | loop fusion | flops 31629312 | bytes 10957824 | tf_op jit(solution)/shard_map/convert.2
  34.2 0.2 pad_maximum_fusion
  34.4 2.7 %gather_fusion = bf16[128,2,16,384]{3,2,1,0:T(8,128)(2,1)} fusion(bf16[2,66,16,384]{3,2,1,0:T(8,128)(2,1)S(1)} %pad_maximum_fusion, s32[1024]{0:T(1024)S(1)} %pad_clamp_fusion), kind=kCustom, calls=%fused_computation | custom fusion | bytes 6291968 | tf_op jit(solution)/shard_map/jit(_take)/gather | solution.py:52
  37.1 2.2 %copy.24 = bf16[2,128,16,384]{3,2,1,0:T(8,128)(2,1)S(1)} copy(bf16[2,128,16,384]{3,2,0,1:T(8,128)(2,1)} %bitcast.89) | data formatting | bytes 6291456 | tf_op jit(solution)/shard_map/jit(_take)/gather | solution.py:52
  39.3 0.7 select_select_fusion
  40.0 2.0 %copy.25 = bf16[2,4,32,16,384]{4,3,2,0,1:T(8,128)(2,1)} copy(bf16[2,4,32,16,384]{4,3,2,1,0:T(8,128)(2,1)S(1)} %select_select_fusion) | data formatting | bytes 6291456 | tf_op jit(solution)/shard_map/jit(_where)/select_n | solution.py:54
  42.0 6.0 %all-to-all-start = ((bf16[2,4,32,16,384]{4,3,2,0,1:T(8,128)(2,1)}), bf16[2,4,32,16,384]{4,3,2,0,1:T(8,128)(2,1)S(1)}, u32[]{:S(2)}, u32[]{:S(2)}) async-start(bf16[2,4,32,16,384]{4,3,2,0,1:T(8,128)(2,1)} %copy.25), calls=%async_computation | async-start | bytes 6291456 | tf_op jit(solution)/shard_map/all_to_all | solution.py:68
  48.0 0.0 all-gather.2.cloned.1.call-start
  48.0 0.7 all-gather.2.cloned.1.call-update
  48.7 68.8 %all-to-all-done = bf16[2,4,32,16,384]{4,3,2,0,1:T(8,128)(2,1)S(1)} async-done(((bf16[2,4,32,16,384]{4,3,2,0,1:T(8,128)(2,1)}), bf16[2,4,32,16,384]{4,3,2,0,1:T(8,128)(2,1)S(1)}, u32[]{:S(2)}, u32[]{:S(2)}) %all-to-all-start) | async-done | bytes 3145760 | tf_op jit(solution)/shard_map/all_to_all | solution.py:68
  117.4 0.6 copy.26
  118.0 3.5 %copy.27 = bf16[2,1,32,64,384]{4,2,0,1,3:T(8,128)(2,1)} copy(bf16[2,1,32,64,384]{4,3,2,0,1:T(8,128)(2,1)S(1)} %bitcast.90) | data formatting | bytes 6291456 | tf_op jit(solution)/shard_map/all_to_all | solution.py:68
  121.5 0.0 copy-start.1
  121.5 4.0 %all-to-all-start.1 = ((bf16[2,1,32,64,384]{4,2,0,1,3:T(8,128)(2,1)}), bf16[2,1,32,64,384]{4,2,0,1,3:T(8,128)(2,1)S(1)}, u32[]{:S(2)}, u32[]{:S(2)}) async-start(bf16[2,1,32,64,384]{4,2,0,1,3:T(8,128)(2,1)} %copy.27), calls=%async_computation.1 | async-start | bytes 6291456 | tf_op jit(solution)/shard_map/all_to_all | solution.py:67
  125.6 0.0 copy-done.1
  125.6 36.7 %all-to-all-done.1 = bf16[2,1,32,64,384]{4,2,0,1,3:T(8,128)(2,1)S(1)} async-done(((bf16[2,1,32,64,384]{4,2,0,1,3:T(8,128)(2,1)}), bf16[2,1,32,64,384]{4,2,0,1,3:T(8,128)(2,1)S(1)}, u32[]{:S(2)}, u32[]{:S(2)}) %all-to-all-start.1) | async-done | bytes 3145760 | tf_op jit(solution)/shard_map/all_to_all | solution.py:67
  162.3 1.8 copy.28
  164.1 0.7 broadcast_multiply_fusion
  164.8 3.5 %copy.35 = f32[1,2,32,4,2,8,384]{6,5,3,4,2,1,0:T(8,128)} copy(f32[1,2,32,4,2,8,384]{6,5,4,3,2,1,0:T(8,128)S(1)} %get-tuple-element.6) | data formatting | bytes 12582912 | tf_op jit(solution)/shard_map/convert_element_type | solution.py:82
  168.3 1.6 copy.31
  169.9 2.7 %mul.425 = bf16[2,32,16,1536]{3,2,1,0:T(8,128)(2,1)} reshape(bf16[2,1,32,16,4,384]{5,4,3,2,0,1:T(4,128)(2,1)S(1)} %copy.31) | data formatting | bytes 6291456 | tf_op jit(solution)/shard_map/mul | solution.py:75
  172.6 0.0 all-gather.2.cloned.1.call-done
  172.6 10.2 %fusion.5 = bf16[2,1,32,16,1536]{4,3,2,1,0:T(8,128)(2,1)} fusion(f32[2,1,32,16,1536]{4,3,2,0,1:T(8,128)} %bitcast.93, bf16[2,32,16,1536]{3,2,1,0:T(8,128)(2,1)} %mul.425, bf16[1,1536,1536]{2,1,0:T(8,128)(2,1)} %all-gather.2.cloned.1.call-done), kind=kOutput, calls=%fused_computation.13 | convolution fusion | flops 4834983936 | bytes 17301504 | tf_op jit(solution)/shard_map/rcstj,cij->rcsti/dot_general | solution.py:76
  (7 shorter events, 0.1 us)
Async XLA Ops:
  6.5 9.5 %copy-start = (bf16[2,66,16,384]{3,2,1,0:T(8,128)(2,1)S(1)}, bf16[2,66,16,384]{3,2,1,0:T(8,128)(2,1)}, u32[]{:S(2)}) copy-start(bf16[2,66,16,384]{3,2,1,0:T(8,128)(2,1)} %param.7) | copy-start | bytes 4866052
  6.5 8.7 %copy-start.4 = (s32[4]{0:T(128)S(1)}, s32[4]{0:T(128)}, u32[]{:S(2)}) copy-start(s32[4]{0:T(128)} %param.9) | copy-start | bytes 52
  6.5 9.2 %copy-start.5 = (s32[4]{0:T(128)S(1)}, s32[4]{0:T(128)}, u32[]{:S(2)}) copy-start(s32[4]{0:T(128)} %param.10) | copy-start | bytes 52
  6.5 9.2 %copy-start.2 = (f32[2,4,9]{2,1,0:T(4,128)S(1)}, f32[2,4,9]{2,1,0:T(4,128)}, u32[]{:S(2)}) copy-start(f32[2,4,9]{2,1,0:T(4,128)} %param.11) | copy-start | bytes 868
  6.5 9.3 %copy-start.3 = (s32[66]{0:T(128)S(1)}, s32[66]{0:T(128)}, u32[]{:S(2)}) copy-start(s32[66]{0:T(128)} %param.8) | copy-start | bytes 796
  8.4 14.3 %collective-permute-start = (bf16[2,66,4,384]{3,2,1,0:T(4,128)(2,1)S(1)}, bf16[2,66,4,384]{3,2,1,0:T(4,128)(2,1)S(1)}, u32[]{:S(2)}, u32[]{:S(2)}) collective-permute-start(bf16[2,66,4,384]{3,2,1,0:T(4,128)(2,1)S(1)} %get-tuple-element.8), channel_id=1, source_target_pairs={{4,0},{8,4},{12,8},{5,1},{9,5},{13,9},{6,2},{10,6},{14,10},{7,3},{... | collective-permute-start | bytes 1216520 | tf_op jit(solution)/shard_map/ppermute | solution.py:20
  9.7 14.2 %collective-permute-start.1 = (bf16[2,66,4,384]{3,2,1,0:T(4,128)(2,1)S(1)}, bf16[2,66,4,384]{3,2,1,0:T(4,128)(2,1)S(1)}, u32[]{:S(2)}, u32[]{:S(2)}) collective-permute-start(bf16[2,66,4,384]{3,2,1,0:T(4,128)(2,1)S(1)} %get-tuple-element.7), channel_id=1, source_target_pairs={{0,4},{4,8},{8,12},{1,5},{5,9},{9,13},{2,6},{6,10},{10,14},{3,7},{... | collective-permute-start | bytes 1216520 | tf_op jit(solution)/shard_map/ppermute | solution.py:18
  42.0 75.4 %all-to-all-start = ((bf16[2,4,32,16,384]{4,3,2,0,1:T(8,128)(2,1)}), bf16[2,4,32,16,384]{4,3,2,0,1:T(8,128)(2,1)S(1)}, u32[]{:S(2)}, u32[]{:S(2)}) async-start(bf16[2,4,32,16,384]{4,3,2,0,1:T(8,128)(2,1)} %copy.25), calls=%async_computation | async-start | bytes 6291456 | tf_op jit(solution)/shard_map/all_to_all | solution.py:68
  48.0 124.7 %all-gather.2.cloned.1.call-start = ((), (), s32[]{:S(2)}) async-start(), calls=%async_computation.2 | async-start | bytes 5898240 | tf_op jit(solution)/shard_map/all_gather | solution.py:79
  121.5 4.0 %copy-start.1 = (s32[16,1536]{1,0:T(8,128)S(1)}, s32[16,1536]{1,0:T(8,128)}, u32[]{:S(2)}) copy-start(s32[16,1536]{1,0:T(8,128)} %param.12) | copy-start | bytes 294916
  121.5 40.7 %all-to-all-start.1 = ((bf16[2,1,32,64,384]{4,2,0,1,3:T(8,128)(2,1)}), bf16[2,1,32,64,384]{4,2,0,1,3:T(8,128)(2,1)S(1)}, u32[]{:S(2)}, u32[]{:S(2)}) async-start(bf16[2,1,32,64,384]{4,2,0,1,3:T(8,128)(2,1)} %copy.27), calls=%async_computation.1 | async-start | bytes 6291456 | tf_op jit(solution)/shard_map/all_to_all | solution.py:67
Sparse Core Ops, SparseCore 0:
  50.3 38.9 all-gather.1
where the time goes:
time: 190 us
  waiting for transfers between devices  114 us (60%)
  local copies, waits for them, and re-layouts  23 us (12%)
  starting transfers between devices  16.8 us (9%)
  between operations  13.6 us (7%)
  other arithmetic  12.4 us (7%)
  matrix products  10.4 us (5%)
    all_to_all x1, waiting for transfers between devices, shards(): lax.all_to_all(slotted, 'tm', split_axis=1, concat_axis=3, tiled=True)  68.8 us
    all_to_all x1, waiting for transfers between devices, shards(): lax.all_to_all(lax.all_to_all(slotted, 'tm', split_axis=1, concat_axis=3,...  36.7 us
    another operation x3, other arithmetic  10.5 us
    dot_general x1, matrix products, shards(): jnp.einsum('rcstj,cij->rcsti', weighted, lax.all_gather(filter_panels, 'f...  10.2 us
    ppermute x1, waiting for transfers between devices, extended(): lax.ppermute(head, axis, [((i + 1) % count, i) for i in range(ends)])  6.46 us
    all_to_all x1, starting transfers between devices, shards(): lax.all_to_all(slotted, 'tm', split_axis=1, concat_axis=3, tiled=True)  5.95 us
    ppermute x1, starting transfers between devices, extended(): lax.ppermute(tail, axis, [(i, (i + 1) % count) for i in range(ends)])  5.58 us
    gather x2, local copies, waits for them, and re-layouts, to_slots(): gathered = jnp.take(per_baseline, input_visibility.reshape(-1), axis=1)  4.87 us
  transfers between devices with their start and end apart: 5, of which 4 were waited for; matrix products, arithmetic and copies ran while one was open for 8% of the time, Pallas kernels for 0%

commit v1 on v0

--- a/solution.py
+++ b/solution.py
@@ -1,10 +1,16 @@
+import functools
+
 import jax
 import jax.numpy as jnp
 from jax import lax
+from jax.experimental import pallas as pl
+from jax.experimental.pallas import tpu as pltpu
 from jax.sharding import PartitionSpec as P
 
 SLOTS = 32
 REACH = 4
+CHUNK = 4
+MESH = pl.DeviceIdType.MESH
 
 
 def extended(cells, sides, width):
@@ -54,7 +60,7 @@
     return jnp.where(live_slot[None, :, :, None, None], gathered, jnp.zeros((), per_baseline.dtype))
 
 
-def shards(
+def plain_shards(
     visibilities, class_ids, class_counts, tap_windows, fringe_taps, flag_mask, filter_panels
 ):
     taps_kept = masked_taps(fringe_taps, tap_windows)
@@ -82,6 +88,307 @@
     return (local_block.astype(jnp.float32) - dayenu_fit).astype(jnp.bfloat16)
 
 
+def tap_matrix(taps_ref, windows_ref, own_class, steps, block):
+    size = 2 * steps
+    out_pos = lax.broadcasted_iota(jnp.int32, (size, size), 0)
+    in_pos = lax.broadcasted_iota(jnp.int32, (size, size), 1)
+
+    def parts(pos):
+        return (pos // (2 * block)) * block + pos % block, (pos // block) % 2
+
+    out_t, out_r = parts(out_pos)
+    in_t, in_r = parts(in_pos)
+    lag = out_t - in_t
+    same = out_r == in_r
+    sign = (out_r - in_r).astype(jnp.float32)
+    matrix = jnp.zeros((size, size), jnp.float32)
+    window = windows_ref[own_class]
+    for offset in range(2 * REACH + 1):
+        keep = jnp.where(abs(offset - REACH) <= window, 1.0, 0.0)
+        real = taps_ref[0, own_class, offset] * keep
+        imag = taps_ref[1, own_class, offset] * keep
+        value = jnp.where(same, real, sign * imag)
+        matrix = jnp.where(lag == offset - REACH, value, matrix)
+    return matrix
+
+
+def kernel(
+    groups,
+    lanes,
+    counts_ref,
+    windows_ref,
+    taps_ref,
+    vis_ref,
+    flag_ref,
+    panel_ref,
+    out_ref,
+    send_z,
+    land_z,
+    send_x,
+    land_x,
+    panels,
+    taps_mat,
+    weighted,
+    result,
+    z_send_sem,
+    z_recv_sem,
+    x_send_sem,
+    x_recv_sem,
+    p_send_sem,
+    p_recv_sem,
+    local_sem,
+    out_sem,
+):
+    my_z = lax.axis_index("tm")
+    my_f = lax.axis_index("freq")
+    chunks = SLOTS // CHUNK
+    block = vis_ref.shape[2]
+    width = vis_ref.shape[3]
+    baselines = vis_ref.shape[1]
+    rows = 2 * CHUNK * block
+
+    def z_peer(d):
+        return lax.rem(my_z + d, groups)
+
+    def f_peer(d):
+        return lax.rem(my_f + d, lanes)
+
+    core_peer = my_f + 1 - 2 * lax.rem(my_f, 2)
+    x_peer = f_peer(2)
+    far_peer = core_peer + 2 - 4 * (core_peer // 2)
+
+    barrier = pltpu.get_barrier_semaphore()
+    for d in range(1, groups):
+        pl.semaphore_signal(barrier, inc=1, device_id={"tm": z_peer(d)}, device_id_type=MESH)
+    for d in range(1, lanes):
+        pl.semaphore_signal(barrier, inc=1, device_id={"freq": f_peer(d)}, device_id_type=MESH)
+    pl.semaphore_wait(barrier, groups + lanes - 2)
+
+    def panel_copy(which, source, owner, target):
+        return pltpu.make_async_remote_copy(
+            src_ref=source,
+            dst_ref=panels.at[owner],
+            send_sem=p_send_sem.at[which],
+            recv_sem=p_recv_sem.at[which],
+            device_id={"freq": target},
+            device_id_type=MESH,
+        )
+
+    to_x = panel_copy(0, panel_ref.at[0], my_f, x_peer)
+    to_core = panel_copy(1, panel_ref.at[0], my_f, core_peer)
+    own_panel = pltpu.make_async_copy(panel_ref.at[0], panels.at[my_f], local_sem)
+
+    def z_copy(q, target, source):
+        return pltpu.make_async_remote_copy(
+            src_ref=send_z.at[q, target],
+            dst_ref=land_z.at[q, source],
+            send_sem=z_send_sem.at[q, target],
+            recv_sem=z_recv_sem.at[q, source],
+            device_id={"tm": target},
+            device_id_type=MESH,
+        )
+
+    def x_copy(q, target, source):
+        return pltpu.make_async_remote_copy(
+            src_ref=send_x.at[q, target],
+            dst_ref=land_x.at[q, source],
+            send_sem=x_send_sem.at[q, target],
+            recv_sem=x_recv_sem.at[q, source],
+            device_id={"freq": target},
+            device_id_type=MESH,
+        )
+
+    def start_of(number):
+        total = 0
+        for i in range(groups):
+            total = total + jnp.where(i < number, counts_ref[i], 0)
+        return total
+
+    starts = [start_of(z_peer(d)) for d in range(groups)]
+
+    def pick(d, q, store):
+        for s in range(CHUNK):
+            row = jnp.minimum(starts[d] + q * CHUNK + s, baselines - 1)
+            for r in range(2):
+                store(r, s, vis_ref[r, row])
+
+    def send_chunk(q, carry):
+        for d in (2, 1, 3):
+            target = z_peer(d)
+
+            def store(r, s, value):
+                send_z[q, target, r, s] = value
+
+            pick(d, q, store)
+            z_copy(q, target, my_z).start()
+        return carry
+
+    send_chunk(0, 0)
+    to_x.start()
+    to_core.start()
+    own_panel.start()
+    lax.fori_loop(1, chunks, send_chunk, 0)
+
+    def keep_chunk(q, carry):
+        def store(r, s, value):
+            land_z[q, my_z, r, s] = value
+
+        pick(0, q, store)
+        return carry
+
+    lax.fori_loop(0, chunks, keep_chunk, 0)
+
+    full = tap_matrix(taps_ref, windows_ref, my_z, groups * block, block)
+    size = 2 * groups * block
+    high = full.astype(jnp.bfloat16)
+    taps_mat[:size, :] = high
+    taps_mat[size:, :] = (full - high.astype(jnp.float32)).astype(jnp.bfloat16)
+    live_count = counts_ref[my_z]
+
+    def filter_chunk(q, carry):
+        for d in range(1, groups):
+            z_copy(q, my_z, z_peer(d)).wait_recv()
+        for s in range(CHUNK):
+            cells = land_z[q, :, :, s].reshape(size, width)
+            both = jnp.dot(taps_mat[...], cells, preferred_element_type=jnp.float32)
+            live = jnp.where(q * CHUNK + s < live_count, 1.0, 0.0)
+            filtered = (both[:size] + both[size:]) * live
+            send_x[q, :, :, s] = filtered.astype(jnp.bfloat16).reshape(lanes, 2, block, width)
+        for d in (2, 1, 3):
+            x_copy(q, f_peer(d), my_f).start()
+        land_x[q, my_f] = send_x[q, my_f]
+        return carry
+
+    def out_copy(q):
+        return pltpu.make_async_copy(
+            result.at[q], out_ref.at[:, 0, pl.ds(q * CHUNK, CHUNK)], out_sem.at[q]
+        )
+
+    def fit_pair(p):
+        for half in range(2):
+            q = 2 * p + half
+            for d in range(1, lanes):
+                x_copy(q, my_f, f_peer(d)).wait_recv()
+            for j in range(lanes):
+                gate = flag_ref[:, j * width : (j + 1) * width].astype(jnp.bfloat16)
+                weighted[half * rows : (half + 1) * rows, j * width : (j + 1) * width] = (
+                    land_x[q, j] * gate
+                ).reshape(rows, width)
+
+        def one_block(i, carry):
+            fit = lax.dot_general(
+                weighted[...],
+                panels[i],
+                (((1,), (1,)), ((), ())),
+                preferred_element_type=jnp.float32,
+            )
+            columns = pl.ds(pl.multiple_of(i * width, width), width)
+            for half in range(2):
+                q = 2 * p + half
+                slotted = land_x[q, i].astype(jnp.float32).reshape(rows, width)
+                cleaned = (slotted - fit[half * rows : (half + 1) * rows]).astype(jnp.bfloat16)
+                result[q, :, :, :, columns] = cleaned.reshape(2, CHUNK, block, width)
+            return carry
+
+        lax.fori_loop(0, lanes, one_block, 0)
+        for half in range(2):
+            out_copy(2 * p + half).start()
+
+    early = chunks // 2
+    lax.fori_loop(0, early, filter_chunk, 0)
+    panel_copy(0, panel_ref.at[0], x_peer, my_f).wait_recv()
+    forward = panel_copy(2, panels.at[x_peer], x_peer, core_peer)
+    forward.start()
+    filter_chunk(early, 0)
+    panel_copy(1, panel_ref.at[0], core_peer, my_f).wait_recv()
+    panel_copy(2, panel_ref.at[0], far_peer, my_f).wait_recv()
+    own_panel.wait()
+    fit_pair(0)
+
+    def late(p, carry):
+        filter_chunk(early + p, 0)
+        fit_pair(p)
+        return carry
+
+    lax.fori_loop(1, early, late, 0)
+
+    def finish(q, carry):
+        out_copy(q).wait()
+        for d in range(1, groups):
+            z_copy(q, z_peer(d), my_z).wait_send()
+        for d in range(1, lanes):
+            x_copy(q, f_peer(d), my_f).wait_send()
+        return carry
+
+    lax.fori_loop(0, chunks, finish, 0)
+    to_x.wait_send()
+    to_core.wait_send()
+    forward.wait_send()
+
+
+def kernel_shards(
+    groups, lanes, visibilities, class_ids, class_counts, tap_windows, fringe_taps, flag_mask, filter_panels
+):
+    block, width = visibilities.shape[2:]
+    channels = lanes * width
+    chunks = SLOTS // CHUNK
+    size = 2 * groups * block
+    bf16 = jnp.bfloat16
+    smem = pl.BlockSpec(memory_space=pltpu.SMEM)
+    vmem = pl.BlockSpec(memory_space=pltpu.VMEM)
+    hbm = pl.BlockSpec(memory_space=pl.ANY)
+    dma = pltpu.SemaphoreType.DMA
+    return pl.pallas_call(
+        functools.partial(kernel, groups, lanes),
+        out_shape=jax.ShapeDtypeStruct((2, 1, SLOTS, block, channels), bf16),
+        in_specs=[smem, smem, smem, vmem, vmem, hbm],
+        out_specs=hbm,
+        scratch_shapes=[
+            pltpu.VMEM((chunks, groups, 2, CHUNK, block, width), bf16),
+            pltpu.VMEM((chunks, groups, 2, CHUNK, block, width), bf16),
+            pltpu.VMEM((chunks, lanes, 2, CHUNK, block, width), bf16),
+            pltpu.VMEM((chunks, lanes, 2, CHUNK, block, width), bf16),
+            pltpu.VMEM((lanes, width, channels), bf16),
+            pltpu.VMEM((2 * size, size), bf16),
+            pltpu.VMEM((4 * CHUNK * block, channels), bf16),
+            pltpu.VMEM((chunks, 2, CHUNK, block, channels), bf16),
+            dma((chunks, groups)),
+            dma((chunks, groups)),
+            dma((chunks, lanes)),
+            dma((chunks, lanes)),
+            dma((3,)),
+            dma((3,)),
+            dma,
+            dma((chunks,)),
+        ],
+        compiler_params=pltpu.CompilerParams(
+            collective_id=0, has_side_effects=True, vmem_limit_bytes=44 * 2**20
+        ),
+        cost_estimate=pl.CostEstimate(
+            flops=2 * 2 * SLOTS * block * channels * channels,
+            bytes_accessed=4 * SLOTS * block * channels * 2,
+            transcendentals=0,
+        ),
+    )(class_counts, tap_windows, fringe_taps, visibilities, flag_mask, filter_panels)
+
+
+def shards(*arrays):
+    visibilities, panels = arrays[0], arrays[6]
+    groups, lanes = lax.axis_size("tm"), lax.axis_size("freq")
+    block, width = visibilities.shape[2:]
+    fits = (
+        groups == 4
+        and lanes == 4
+        and panels.shape[0] == 1
+        and arrays[5].shape[0] == block
+        and block % 16 == 0
+        and width % 128 == 0
+    )
+    if fits:
+        return kernel_shards(groups, lanes, *arrays)
+    return plain_shards(*arrays)
+
+
 def solution(mesh):
     return jax.shard_map(
         shards,

time: 190 us -> 90.5 us (0.48)
  waiting for transfers between devices: 114 us -> 0 us
  Pallas kernels: 0 us -> 82.3 us
  starting transfers between devices: 16.8 us -> 0 us
  local copies, waits for them, and re-layouts: 23 us -> 7.25 us
  between operations: 13.6 us -> 0.02 us
  other arithmetic: 12.4 us -> 0 us
  matrix products: 10.4 us -> 0 us
    all_to_all x2 -> x0, waiting for transfers between devices: 105 us -> none  [the longest x1 68.8 us: shards(): lax.all_to_all(slotted, 'tm', split_axis=1, concat_axis=3, tiled=True)]
    pallas_call x0 -> x1, Pallas kernels: none -> 82.3 us  [kernel_shards(): pl.pallas_call(functools.partial(kernel, groups, lanes), out_shape=jax.Sh...]
    another operation x4 -> x0, other arithmetic: 10.7 us -> none
    dot_general x2 -> x0, matrix products: 10.4 us -> none  [the longest x1 10.2 us: shards(): jnp.einsum('rcstj,cij->rcsti', weighted, lax.all_gather(filter_panels, 'f...]
    all_to_all x2 -> x0, starting transfers between devices: 9.97 us -> none  [the longest x1 5.95 us: shards(): lax.all_to_all(slotted, 'tm', split_axis=1, concat_axis=3, tiled=True)]
    ppermute x2 -> x0, waiting for transfers between devices: 7.36 us -> none  [the longest x1 6.46 us: extended(): lax.ppermute(head, axis, [((i + 1) % count, i) for i in range(ends)])]
    unnamed x13, local copies, waits for them, and re-layouts: 0.19 us -> 7.25 us
    ppermute x2 -> x0, starting transfers between devices: 6.87 us -> none  [the longest x1 5.58 us: extended(): lax.ppermute(tail, axis, [(i, (i + 1) % count) for i in range(ends)])]
  transfers between devices with their start and end apart: 5 -> 0, of which waited for: 4 -> 0; matrix products, arithmetic and copies ran while one was open for 8% -> 0% of each run, Pallas kernels for 0% -> 0%
where the time goes in v1:
time: 90.5 us; the launch traced here: 89.5 us
  Pallas kernels  82.3 us (91%)
  local copies, waits for them, and re-layouts  7.25 us (8%)
    pallas_call x1, Pallas kernels, kernel_shards(): pl.pallas_call(functools.partial(kernel, groups, lanes), out_shape=jax.Sh...  82.3 us
    unnamed x13, local copies, waits for them, and re-layouts  7.25 us

profile of v1, /device:TPU:0, one launch (start us, length us, event | category | flops | bytes accessed | tf_op | source)
XLA Modules:
  0.0 89.5 jit_solution(1257755894760772671)
XLA Ops:
  0.0 0.0 copy-start
  0.0 1.4 %copy-done = bf16[2,66,16,384]{3,2,1,0:T(8,128)(2,1)S(1)} copy-done((bf16[2,66,16,384]{3,2,1,0:T(8,128)(2,1)S(1)}, bf16[2,66,16,384]{3,2,1,0:T(8,128)(2,1)}, u32[]{:S(2)}) %copy-start) | copy-done | bytes 1622040
  1.4 0.0 copy-start.1
  1.4 1.3 %copy-done.1 = bf16[1,384,1536]{2,1,0:T(8,128)(2,1)S(1)} copy-done((bf16[1,384,1536]{2,1,0:T(8,128)(2,1)S(1)}, bf16[1,384,1536]{2,1,0:T(8,128)(2,1)}, u32[]{:S(2)}) %copy-start.1) | copy-done | bytes 1179672
  2.7 0.0 copy-start.2
  2.7 0.9 copy-done.2
  3.6 0.0 copy-start.3
  3.6 0.7 copy-done.3
  4.3 0.0 copy-start.4
  4.3 0.7 copy-done.4
  4.9 0.0 copy-start.5
  4.9 0.7 copy-done.5
  5.6 82.3 %shard_map.64 = bf16[2,1,32,16,1536]{4,3,2,1,0:T(8,128)(2,1)S(1)} custom-call(s32[4]{0:T(128)S(1)} %copy-done.4, s32[4]{0:T(128)S(1)} %copy-done.5, f32[2,4,9]{2,1,0:T(4,128)S(1)} %copy-done.3, bf16[2,66,16,384]{3,2,1,0:T(8,128)(2,1)S(1)} %copy-done, s32[16,1536]{1,0:T(8,128)S(1)} %copy-done.2, bf16[1,384,1536]{2,1,0:T(8,128)(2,1)S(1)} %copy-done.1), custom_call_target="tpu_custom_call" | custom-call | flops 4831838208 | bytes 6291456 | tf_op jit(solution)/shard_map/pallas_call | solution.py:341
  87.9 1.7 %copy.8 = bf16[2,1,32,16,1536]{4,3,2,1,0:T(8,128)(2,1)} copy(bf16[2,1,32,16,1536]{4,3,2,1,0:T(8,128)(2,1)S(1)} %shard_map.64) | data formatting | bytes 6291456
Async XLA Ops:
  0.0 1.4 %copy-start = (bf16[2,66,16,384]{3,2,1,0:T(8,128)(2,1)S(1)}, bf16[2,66,16,384]{3,2,1,0:T(8,128)(2,1)}, u32[]{:S(2)}) copy-start(bf16[2,66,16,384]{3,2,1,0:T(8,128)(2,1)} %vis_ref.1) | copy-start | bytes 4866052
  1.4 1.3 %copy-start.1 = (bf16[1,384,1536]{2,1,0:T(8,128)(2,1)S(1)}, bf16[1,384,1536]{2,1,0:T(8,128)(2,1)}, u32[]{:S(2)}) copy-start(bf16[1,384,1536]{2,1,0:T(8,128)(2,1)} %panel_ref.1) | copy-start | bytes 3538948
  2.7 0.9 copy-start.2
  3.6 0.7 copy-start.3
  4.3 0.7 copy-start.4
  4.9 0.7 copy-start.5

commit v2 on v1

--- a/solution.py
+++ b/solution.py
@@ -9,7 +9,8 @@
 
 SLOTS = 32
 REACH = 4
-CHUNK = 4
+CHUNK = 2
+GROUP = 4
 MESH = pl.DeviceIdType.MESH
 
 
@@ -118,15 +119,17 @@
     counts_ref,
     windows_ref,
     taps_ref,
-    vis_ref,
+    vis_hbm,
     flag_ref,
     panel_ref,
     out_ref,
+    vis_ref,
     send_z,
     land_z,
     send_x,
     land_x,
     panels,
+    panels_t,
     taps_mat,
     weighted,
     result,
@@ -137,6 +140,7 @@
     p_send_sem,
     p_recv_sem,
     local_sem,
+    vis_sem,
     out_sem,
 ):
     my_z = lax.axis_index("tm")
@@ -157,6 +161,9 @@
     x_peer = f_peer(2)
     far_peer = core_peer + 2 - 4 * (core_peer // 2)
 
+    fetch = pltpu.make_async_copy(vis_hbm, vis_ref, vis_sem)
+    fetch.start()
+
     barrier = pltpu.get_barrier_semaphore()
     for d in range(1, groups):
         pl.semaphore_signal(barrier, inc=1, device_id={"tm": z_peer(d)}, device_id_type=MESH)
@@ -223,6 +230,7 @@
             z_copy(q, target, my_z).start()
         return carry
 
+    fetch.wait()
     send_chunk(0, 0)
     to_x.start()
     to_core.start()
@@ -264,53 +272,63 @@
             result.at[q], out_ref.at[:, 0, pl.ds(q * CHUNK, CHUNK)], out_sem.at[q]
         )
 
-    def fit_pair(p):
-        for half in range(2):
-            q = 2 * p + half
+    def fit_chunks(first, count):
+        for h in range(count):
             for d in range(1, lanes):
-                x_copy(q, my_f, f_peer(d)).wait_recv()
+                x_copy(first + h, my_f, f_peer(d)).wait_recv()
             for j in range(lanes):
                 gate = flag_ref[:, j * width : (j + 1) * width].astype(jnp.bfloat16)
-                weighted[half * rows : (half + 1) * rows, j * width : (j + 1) * width] = (
-                    land_x[q, j] * gate
+                weighted[h * rows : (h + 1) * rows, j * width : (j + 1) * width] = (
+                    land_x[first + h, j] * gate
                 ).reshape(rows, width)
 
         def one_block(i, carry):
-            fit = lax.dot_general(
-                weighted[...],
-                panels[i],
-                (((1,), (1,)), ((), ())),
-                preferred_element_type=jnp.float32,
+            fit = jnp.dot(
+                weighted[: count * rows], panels_t[i], preferred_element_type=jnp.float32
             )
             columns = pl.ds(pl.multiple_of(i * width, width), width)
-            for half in range(2):
-                q = 2 * p + half
-                slotted = land_x[q, i].astype(jnp.float32).reshape(rows, width)
-                cleaned = (slotted - fit[half * rows : (half + 1) * rows]).astype(jnp.bfloat16)
-                result[q, :, :, :, columns] = cleaned.reshape(2, CHUNK, block, width)
+            for h in range(count):
+                slotted = land_x[first + h, i].astype(jnp.float32).reshape(rows, width)
+                cleaned = (slotted - fit[h * rows : (h + 1) * rows]).astype(jnp.bfloat16)
+                result[first + h, :, :, :, columns] = cleaned.reshape(2, CHUNK, block, width)
             return carry
 
         lax.fori_loop(0, lanes, one_block, 0)
-        for half in range(2):
-            out_copy(2 * p + half).start()
+        for h in range(count):
+            out_copy(first + h).start()
+
+    def turn(i, carry):
+        panels_t[i] = panels[i].T
+        return carry
 
     early = chunks // 2
     lax.fori_loop(0, early, filter_chunk, 0)
     panel_copy(0, panel_ref.at[0], x_peer, my_f).wait_recv()
     forward = panel_copy(2, panels.at[x_peer], x_peer, core_peer)
     forward.start()
-    filter_chunk(early, 0)
+    lax.fori_loop(early, early + 1, filter_chunk, 0)
     panel_copy(1, panel_ref.at[0], core_peer, my_f).wait_recv()
     panel_copy(2, panel_ref.at[0], far_peer, my_f).wait_recv()
     own_panel.wait()
-    fit_pair(0)
-
-    def late(p, carry):
-        filter_chunk(early + p, 0)
-        fit_pair(p)
-        return carry
-
-    lax.fori_loop(1, early, late, 0)
+    lax.fori_loop(0, lanes, turn, 0)
+
+    def late(g, carry):
+        fit_chunks(g * GROUP, GROUP)
+        lax.fori_loop(early + 1 + 2 * g, early + 3 + 2 * g, filter_chunk, 0)
+        return carry
+
+    groups_done = chunks // GROUP - 1
+    lax.fori_loop(0, groups_done, late, 0)
+    done = groups_done * GROUP
+    lax.fori_loop(early + 1 + 2 * groups_done, chunks - 1, filter_chunk, 0)
+    fit_chunks(done, 2)
+    lax.fori_loop(chunks - 1, chunks, filter_chunk, 0)
+
+    def last(q, carry):
+        fit_chunks(q, 1)
+        return carry
+
+    lax.fori_loop(done + 2, chunks, last, 0)
 
     def finish(q, carry):
         out_copy(q).wait()
@@ -341,16 +359,18 @@
     return pl.pallas_call(
         functools.partial(kernel, groups, lanes),
         out_shape=jax.ShapeDtypeStruct((2, 1, SLOTS, block, channels), bf16),
-        in_specs=[smem, smem, smem, vmem, vmem, hbm],
+        in_specs=[smem, smem, smem, hbm, vmem, hbm],
         out_specs=hbm,
         scratch_shapes=[
+            pltpu.VMEM(visibilities.shape, bf16),
             pltpu.VMEM((chunks, groups, 2, CHUNK, block, width), bf16),
             pltpu.VMEM((chunks, groups, 2, CHUNK, block, width), bf16),
             pltpu.VMEM((chunks, lanes, 2, CHUNK, block, width), bf16),
             pltpu.VMEM((chunks, lanes, 2, CHUNK, block, width), bf16),
             pltpu.VMEM((lanes, width, channels), bf16),
+            pltpu.VMEM((lanes, channels, width), bf16),
             pltpu.VMEM((2 * size, size), bf16),
-            pltpu.VMEM((4 * CHUNK * block, channels), bf16),
+            pltpu.VMEM((GROUP * 2 * CHUNK * block, channels), bf16),
             pltpu.VMEM((chunks, 2, CHUNK, block, channels), bf16),
             dma((chunks, groups)),
             dma((chunks, groups)),
@@ -359,10 +379,11 @@
             dma((3,)),
             dma((3,)),
             dma,
+            dma,
             dma((chunks,)),
         ],
         compiler_params=pltpu.CompilerParams(
-            collective_id=0, has_side_effects=True, vmem_limit_bytes=44 * 2**20
+            collective_id=0, has_side_effects=True, vmem_limit_bytes=60 * 2**20
         ),
         cost_estimate=pl.CostEstimate(
             flops=2 * 2 * SLOTS * block * channels * channels,

time: 90.5 us -> 93.3 us (1.031)
  Pallas kernels: 82.3 us -> 89.3 us
  local copies, waits for them, and re-layouts: 7.25 us -> 3.76 us
    pallas_call x1, Pallas kernels: 82.3 us -> 89.3 us  [kernel_shards(): pl.pallas_call(functools.partial(kernel, groups, lanes), out_shape=jax.Sh...]
    unnamed x13 -> x1, local copies, waits for them, and re-layouts: 7.25 us -> 3.76 us
where the time goes in v2:
time: 93.3 us; the launch traced here: 93.1 us
  Pallas kernels  89.3 us (96%)
  local copies, waits for them, and re-layouts  3.76 us (4%)
    pallas_call x1, Pallas kernels, kernel_shards(): pl.pallas_call(functools.partial(kernel, groups, lanes), out_shape=jax.Sh...  89.3 us
    unnamed x1, local copies, waits for them, and re-layouts  3.76 us

profile of v2, /device:TPU:0, one launch (start us, length us, event | category | flops | bytes accessed | tf_op | source)
XLA Modules:
  0.0 93.1 jit_solution(14813917341578778349)
XLA Ops:
  0.0 89.3 %shard_map.64 = bf16[2,1,32,16,1536]{4,3,2,1,0:T(8,128)(2,1)} custom-call(s32[4]{0:T(128)} %counts_ref.1, s32[4]{0:T(128)} %windows_ref.1, f32[2,4,9]{2,1,0:T(4,128)} %taps_ref.1, bf16[2,66,16,384]{3,2,1,0:T(8,128)(2,1)} %vis_hbm.1, s32[16,1536]{1,0:T(8,128)} %flag_ref.1, bf16[1,384,1536]{2,1,0:T(8,128)(2,1)} %panel_ref.1), custom_call_target="tpu_custom_call" | custom-call | flops 4831838208 | bytes 6291456 | tf_op jit(solution)/shard_map/pallas_call | solution.py:359
  89.3 3.8 %copy.8 = bf16[2,1,32,16,1536]{4,3,2,1,0:T(8,128)(2,1)} copy(bf16[2,1,32,16,1536]{4,3,2,1,0:T(8,128)(2,1)} %shard_map.64) | data formatting | bytes 6291456

commit v3 on v2

--- a/solution.py
+++ b/solution.py
@@ -9,8 +9,8 @@
 
 SLOTS = 32
 REACH = 4
-CHUNK = 2
-GROUP = 4
+CHUNK = 4
+GROUP = 2
 MESH = pl.DeviceIdType.MESH
 
 
@@ -116,13 +116,17 @@
 def kernel(
     groups,
     lanes,
+    counts_hbm,
+    windows_hbm,
+    taps_hbm,
+    vis_hbm,
+    flag_hbm,
+    panel_ref,
+    out_ref,
     counts_ref,
     windows_ref,
     taps_ref,
-    vis_hbm,
     flag_ref,
-    panel_ref,
-    out_ref,
     vis_ref,
     send_z,
     land_z,
@@ -140,7 +144,7 @@
     p_send_sem,
     p_recv_sem,
     local_sem,
-    vis_sem,
+    fetch_sem,
     out_sem,
 ):
     my_z = lax.axis_index("tm")
@@ -161,8 +165,20 @@
     x_peer = f_peer(2)
     far_peer = core_peer + 2 - 4 * (core_peer // 2)
 
-    fetch = pltpu.make_async_copy(vis_hbm, vis_ref, vis_sem)
-    fetch.start()
+    fetches = [
+        pltpu.make_async_copy(source, target, fetch_sem.at[i])
+        for i, (source, target) in enumerate(
+            (
+                (counts_hbm, counts_ref),
+                (vis_hbm, vis_ref),
+                (taps_hbm, taps_ref),
+                (windows_hbm, windows_ref),
+                (flag_hbm, flag_ref),
+            )
+        )
+    ]
+    for fetch in fetches:
+        fetch.start()
 
     barrier = pltpu.get_barrier_semaphore()
     for d in range(1, groups):
@@ -211,37 +227,65 @@
             total = total + jnp.where(i < number, counts_ref[i], 0)
         return total
 
-    starts = [start_of(z_peer(d)) for d in range(groups)]
-
-    def pick(d, q, store):
+    def pick(number, q, store):
+        first = start_of(number)
         for s in range(CHUNK):
-            row = jnp.minimum(starts[d] + q * CHUNK + s, baselines - 1)
+            row = jnp.minimum(first + q * CHUNK + s, baselines - 1)
             for r in range(2):
                 store(r, s, vis_ref[r, row])
 
-    def send_chunk(q, carry):
-        for d in (2, 1, 3):
-            target = z_peer(d)
-
-            def store(r, s, value):
-                send_z[q, target, r, s] = value
-
-            pick(d, q, store)
-            z_copy(q, target, my_z).start()
-        return carry
-
-    fetch.wait()
-    send_chunk(0, 0)
+    def send_chunk(q, target):
+        def store(r, s, value):
+            send_z[q, target, r, s] = value
+
+        pick(target, q, store)
+        z_copy(q, target, my_z).start()
+
+    near = my_z + 1 - 2 * lax.rem(my_z, 2)
+    across = (z_peer(2), lax.rem(near + 2, groups))
+    inner = my_z % 3 != 0
+
+    def send_near(q, carry):
+        send_chunk(q, near)
+        return carry
+
+    def send_across(q, carry):
+        for target in across:
+            send_chunk(q, target)
+
+        @pl.when(jnp.logical_and(inner, q >= chunks // 2))
+        def _():
+            send_chunk(2 * q - chunks, near)
+            send_chunk(2 * q - chunks + 1, near)
+
+        return carry
+
+    fetches[0].wait()
+    fetches[1].wait()
+    send_chunk(0, jnp.where(inner, across[0], near))
     to_x.start()
     to_core.start()
     own_panel.start()
-    lax.fori_loop(1, chunks, send_chunk, 0)
+
+    @pl.when(inner)
+    def _():
+        send_chunk(0, across[1])
+
+    @pl.when(jnp.logical_not(inner))
+    def _():
+        lax.fori_loop(1, chunks, send_near, 0)
+        for target in across:
+            send_chunk(0, target)
+
+    lax.fori_loop(1, chunks, send_across, 0)
+    for fetch in fetches[2:]:
+        fetch.wait()
 
     def keep_chunk(q, carry):
         def store(r, s, value):
             land_z[q, my_z, r, s] = value
 
-        pick(0, q, store)
+        pick(my_z, q, store)
         return carry
 
     lax.fori_loop(0, chunks, keep_chunk, 0)
@@ -314,21 +358,16 @@
 
     def late(g, carry):
         fit_chunks(g * GROUP, GROUP)
-        lax.fori_loop(early + 1 + 2 * g, early + 3 + 2 * g, filter_chunk, 0)
-        return carry
-
-    groups_done = chunks // GROUP - 1
-    lax.fori_loop(0, groups_done, late, 0)
-    done = groups_done * GROUP
-    lax.fori_loop(early + 1 + 2 * groups_done, chunks - 1, filter_chunk, 0)
-    fit_chunks(done, 2)
-    lax.fori_loop(chunks - 1, chunks, filter_chunk, 0)
+        lax.fori_loop(early + 1 + g, early + 2 + g, filter_chunk, 0)
+        return carry
+
+    lax.fori_loop(0, early - 1, late, 0)
 
     def last(q, carry):
         fit_chunks(q, 1)
         return carry
 
-    lax.fori_loop(done + 2, chunks, last, 0)
+    lax.fori_loop(chunks - GROUP, chunks, last, 0)
 
     def finish(q, carry):
         out_copy(q).wait()
@@ -352,16 +391,18 @@
     chunks = SLOTS // CHUNK
     size = 2 * groups * block
     bf16 = jnp.bfloat16
-    smem = pl.BlockSpec(memory_space=pltpu.SMEM)
-    vmem = pl.BlockSpec(memory_space=pltpu.VMEM)
-    hbm = pl.BlockSpec(memory_space=pl.ANY)
+    hbm = pl.BlockSpec(memory_space=pltpu.HBM)
     dma = pltpu.SemaphoreType.DMA
     return pl.pallas_call(
         functools.partial(kernel, groups, lanes),
         out_shape=jax.ShapeDtypeStruct((2, 1, SLOTS, block, channels), bf16),
-        in_specs=[smem, smem, smem, hbm, vmem, hbm],
-        out_specs=hbm,
+        in_specs=[hbm] * 6,
+        out_specs=pl.BlockSpec(memory_space=pl.ANY),
         scratch_shapes=[
+            pltpu.SMEM(class_counts.shape, jnp.int32),
+            pltpu.SMEM(tap_windows.shape, jnp.int32),
+            pltpu.SMEM(fringe_taps.shape, jnp.float32),
+            pltpu.VMEM(flag_mask.shape, jnp.int32),
             pltpu.VMEM(visibilities.shape, bf16),
             pltpu.VMEM((chunks, groups, 2, CHUNK, block, width), bf16),
             pltpu.VMEM((chunks, groups, 2, CHUNK, block, width), bf16),
@@ -379,7 +420,7 @@
             dma((3,)),
             dma((3,)),
             dma,
-            dma,
+            dma((5,)),
             dma((chunks,)),
         ],
         compiler_params=pltpu.CompilerParams(

time: 93.3 us -> 86.1 us (0.923); the launches traced: 93.1 us -> 84.7 us
  Pallas kernels: 89.3 us -> 80.9 us
    pallas_call x1, Pallas kernels: 89.3 us -> 80.9 us  [kernel_shards(): pl.pallas_call(functools.partial(kernel, groups, lanes), out_shape=jax.Sh...]
where the time goes in v3:
time: 86.1 us; the launch traced here: 84.7 us
  Pallas kernels  80.9 us (94%)
  local copies, waits for them, and re-layouts  3.76 us (4%)
    pallas_call x1, Pallas kernels, kernel_shards(): pl.pallas_call(functools.partial(kernel, groups, lanes), out_shape=jax.Sh...  80.9 us
    unnamed x1, local copies, waits for them, and re-layouts  3.76 us

profile of v3, /device:TPU:0, one launch (start us, length us, event | category | flops | bytes accessed | tf_op | source)
XLA Modules:
  0.0 84.7 jit_solution(18210642440618509216)
XLA Ops:
  0.0 80.9 %shard_map.64 = bf16[2,1,32,16,1536]{4,3,2,1,0:T(8,128)(2,1)} custom-call(s32[4]{0:T(128)} %counts_hbm.1, s32[4]{0:T(128)} %windows_hbm.1, f32[2,4,9]{2,1,0:T(4,128)} %taps_hbm.1, bf16[2,66,16,384]{3,2,1,0:T(8,128)(2,1)} %vis_hbm.1, s32[16,1536]{1,0:T(8,128)} %flag_hbm.1, bf16[1,384,1536]{2,1,0:T(8,128)(2,1)} %panel_ref.1), custom_call_target="tpu_custom_call" | custom-call | flops 4831838208 | bytes 6291456 | tf_op jit(solution)/shard_map/pallas_call | solution.py:396
  80.9 3.8 %copy.8 = bf16[2,1,32,16,1536]{4,3,2,1,0:T(8,128)(2,1)} copy(bf16[2,1,32,16,1536]{4,3,2,1,0:T(8,128)(2,1)} %shard_map.64) | data formatting | bytes 6291456

commit v4 on v3

--- a/solution.py
+++ b/solution.py
@@ -9,8 +9,9 @@
 
 SLOTS = 32
 REACH = 4
-CHUNK = 4
-GROUP = 2
+CHUNK = 2
+GROUP = 4
+AHEAD = 6
 MESH = pl.DeviceIdType.MESH
 
 
@@ -245,39 +246,24 @@
     across = (z_peer(2), lax.rem(near + 2, groups))
     inner = my_z % 3 != 0
 
-    def send_near(q, carry):
+    def send_all(q, carry):
         send_chunk(q, near)
-        return carry
-
-    def send_across(q, carry):
         for target in across:
             send_chunk(q, target)
-
-        @pl.when(jnp.logical_and(inner, q >= chunks // 2))
-        def _():
-            send_chunk(2 * q - chunks, near)
-            send_chunk(2 * q - chunks + 1, near)
-
         return carry
 
     fetches[0].wait()
     fetches[1].wait()
-    send_chunk(0, jnp.where(inner, across[0], near))
+    send_all(0, 0)
     to_x.start()
     to_core.start()
     own_panel.start()
-
-    @pl.when(inner)
-    def _():
-        send_chunk(0, across[1])
+    lax.fori_loop(1, AHEAD, send_all, 0)
 
     @pl.when(jnp.logical_not(inner))
     def _():
-        lax.fori_loop(1, chunks, send_near, 0)
-        for target in across:
-            send_chunk(0, target)
-
-    lax.fori_loop(1, chunks, send_across, 0)
+        lax.fori_loop(AHEAD, chunks, send_all, 0)
+
     for fetch in fetches[2:]:
         fetch.wait()
 
@@ -309,6 +295,11 @@
         for d in (2, 1, 3):
             x_copy(q, f_peer(d), my_f).start()
         land_x[q, my_f] = send_x[q, my_f]
+
+        @pl.when(jnp.logical_and(inner, q + AHEAD < chunks))
+        def _():
+            send_all(q + AHEAD, 0)
+
         return carry
 
     def out_copy(q):
@@ -341,33 +332,44 @@
         for h in range(count):
             out_copy(first + h).start()
 
-    def turn(i, carry):
+    def turn(i):
         panels_t[i] = panels[i].T
-        return carry
-
-    early = chunks // 2
-    lax.fori_loop(0, early, filter_chunk, 0)
+
+    def filter_chunks(first, last):
+        lax.fori_loop(first, last, filter_chunk, 0)
+
+    late = chunks - chunks // GROUP - 2
+    filter_chunks(0, 1)
+    own_panel.wait()
+    turn(my_f)
+    filter_chunks(1, 3)
+    panel_copy(1, panel_ref.at[0], core_peer, my_f).wait_recv()
+    turn(core_peer)
+    filter_chunks(3, late)
     panel_copy(0, panel_ref.at[0], x_peer, my_f).wait_recv()
     forward = panel_copy(2, panels.at[x_peer], x_peer, core_peer)
     forward.start()
-    lax.fori_loop(early, early + 1, filter_chunk, 0)
-    panel_copy(1, panel_ref.at[0], core_peer, my_f).wait_recv()
+    turn(x_peer)
+    filter_chunks(late, late + 1)
     panel_copy(2, panel_ref.at[0], far_peer, my_f).wait_recv()
-    own_panel.wait()
-    lax.fori_loop(0, lanes, turn, 0)
-
-    def late(g, carry):
+    turn(far_peer)
+    filter_chunks(late + 1, late + 2)
+
+    def fit_group(g, carry):
         fit_chunks(g * GROUP, GROUP)
-        lax.fori_loop(early + 1 + g, early + 2 + g, filter_chunk, 0)
-        return carry
-
-    lax.fori_loop(0, early - 1, late, 0)
-
-    def last(q, carry):
+        filter_chunk(late + 2 + g, 0)
+        return carry
+
+    full_groups = chunks // GROUP - 1
+    lax.fori_loop(0, full_groups, fit_group, 0)
+    fit_chunks(full_groups * GROUP, GROUP // 2)
+    filter_chunks(late + 2 + full_groups, chunks)
+
+    def fit_one(q, carry):
         fit_chunks(q, 1)
         return carry
 
-    lax.fori_loop(chunks - GROUP, chunks, last, 0)
+    lax.fori_loop(full_groups * GROUP + GROUP // 2, chunks, fit_one, 0)
 
     def finish(q, carry):
         out_copy(q).wait()

time: 86.1 us -> 87.8 us (1.020); the launches traced: 84.7 us -> 87.7 us
  Pallas kernels: 80.9 us -> 83.9 us
    pallas_call x1, Pallas kernels: 80.9 us -> 83.9 us  [kernel_shards(): pl.pallas_call(functools.partial(kernel, groups, lanes), out_shape=jax.Sh...]
where the time goes in v4:
time: 87.8 us; the launch traced here: 87.7 us
  Pallas kernels  83.9 us (96%)
  local copies, waits for them, and re-layouts  3.76 us (4%)
    pallas_call x1, Pallas kernels, kernel_shards(): pl.pallas_call(functools.partial(kernel, groups, lanes), out_shape=jax.Sh...  83.9 us
    unnamed x1, local copies, waits for them, and re-layouts  3.76 us

profile of v4, /device:TPU:0, one launch (start us, length us, event | category | flops | bytes accessed | tf_op | source)
XLA Modules:
  0.0 87.7 jit_solution(8074537158227156216)
XLA Ops:
  0.0 83.9 %shard_map.64 = bf16[2,1,32,16,1536]{4,3,2,1,0:T(8,128)(2,1)} custom-call(s32[4]{0:T(128)} %counts_hbm.1, s32[4]{0:T(128)} %windows_hbm.1, f32[2,4,9]{2,1,0:T(4,128)} %taps_hbm.1, bf16[2,66,16,384]{3,2,1,0:T(8,128)(2,1)} %vis_hbm.1, s32[16,1536]{1,0:T(8,128)} %flag_hbm.1, bf16[1,384,1536]{2,1,0:T(8,128)(2,1)} %panel_ref.1), custom_call_target="tpu_custom_call" | custom-call | flops 4831838208 | bytes 6291456 | tf_op jit(solution)/shard_map/pallas_call | solution.py:398
  83.9 3.8 %copy.8 = bf16[2,1,32,16,1536]{4,3,2,1,0:T(8,128)(2,1)} copy(bf16[2,1,32,16,1536]{4,3,2,1,0:T(8,128)(2,1)} %shard_map.64) | data formatting | bytes 6291456

commit v5 on v4

--- a/solution.py
+++ b/solution.py
@@ -9,9 +9,9 @@
 
 SLOTS = 32
 REACH = 4
-CHUNK = 2
-GROUP = 4
-AHEAD = 6
+CHUNK = 4
+GROUP = 2
+AHEAD = 3
 MESH = pl.DeviceIdType.MESH
 
 
@@ -244,7 +244,6 @@
 
     near = my_z + 1 - 2 * lax.rem(my_z, 2)
     across = (z_peer(2), lax.rem(near + 2, groups))
-    inner = my_z % 3 != 0
 
     def send_all(q, carry):
         send_chunk(q, near)
@@ -259,10 +258,6 @@
     to_core.start()
     own_panel.start()
     lax.fori_loop(1, AHEAD, send_all, 0)
-
-    @pl.when(jnp.logical_not(inner))
-    def _():
-        lax.fori_loop(AHEAD, chunks, send_all, 0)
 
     for fetch in fetches[2:]:
         fetch.wait()
@@ -296,7 +291,7 @@
             x_copy(q, f_peer(d), my_f).start()
         land_x[q, my_f] = send_x[q, my_f]
 
-        @pl.when(jnp.logical_and(inner, q + AHEAD < chunks))
+        @pl.when(q + AHEAD < chunks)
         def _():
             send_all(q + AHEAD, 0)
 
@@ -338,38 +333,35 @@
     def filter_chunks(first, last):
         lax.fori_loop(first, last, filter_chunk, 0)
 
-    late = chunks - chunks // GROUP - 2
+    half = chunks // 2
     filter_chunks(0, 1)
     own_panel.wait()
     turn(my_f)
-    filter_chunks(1, 3)
+    filter_chunks(1, 2)
     panel_copy(1, panel_ref.at[0], core_peer, my_f).wait_recv()
     turn(core_peer)
-    filter_chunks(3, late)
+    filter_chunks(2, half + 1)
     panel_copy(0, panel_ref.at[0], x_peer, my_f).wait_recv()
     forward = panel_copy(2, panels.at[x_peer], x_peer, core_peer)
     forward.start()
     turn(x_peer)
-    filter_chunks(late, late + 1)
+    filter_chunks(half + 1, half + 2)
     panel_copy(2, panel_ref.at[0], far_peer, my_f).wait_recv()
     turn(far_peer)
-    filter_chunks(late + 1, late + 2)
 
     def fit_group(g, carry):
         fit_chunks(g * GROUP, GROUP)
-        filter_chunk(late + 2 + g, 0)
-        return carry
-
-    full_groups = chunks // GROUP - 1
-    lax.fori_loop(0, full_groups, fit_group, 0)
-    fit_chunks(full_groups * GROUP, GROUP // 2)
-    filter_chunks(late + 2 + full_groups, chunks)
+        return carry
 
     def fit_one(q, carry):
         fit_chunks(q, 1)
         return carry
 
-    lax.fori_loop(full_groups * GROUP + GROUP // 2, chunks, fit_one, 0)
+    lax.fori_loop(0, 1, fit_group, 0)
+    filter_chunks(half + 2, chunks - 1)
+    lax.fori_loop(1, chunks // GROUP - 1, fit_group, 0)
+    filter_chunks(chunks - 1, chunks)
+    lax.fori_loop(chunks - GROUP, chunks, fit_one, 0)
 
     def finish(q, carry):
         out_copy(q).wait()

time: 87.8 us -> 86.1 us (0.981)
  Pallas kernels: 83.9 us -> 81.6 us
    pallas_call x1, Pallas kernels: 83.9 us -> 81.6 us  [kernel_shards(): pl.pallas_call(functools.partial(kernel, groups, lanes), out_shape=jax.Sh...]
where the time goes in v5:
time: 86.1 us; the launch traced here: 85.3 us
  Pallas kernels  81.6 us (95%)
  local copies, waits for them, and re-layouts  3.76 us (4%)
    pallas_call x1, Pallas kernels, kernel_shards(): pl.pallas_call(functools.partial(kernel, groups, lanes), out_shape=jax.Sh...  81.6 us
    unnamed x1, local copies, waits for them, and re-layouts  3.76 us

profile of v5, /device:TPU:0, one launch (start us, length us, event | category | flops | bytes accessed | tf_op | source)
XLA Modules:
  0.0 85.3 jit_solution(18289197433059322317)
XLA Ops:
  0.0 81.6 %shard_map.64 = bf16[2,1,32,16,1536]{4,3,2,1,0:T(8,128)(2,1)} custom-call(s32[4]{0:T(128)} %counts_hbm.1, s32[4]{0:T(128)} %windows_hbm.1, f32[2,4,9]{2,1,0:T(4,128)} %taps_hbm.1, bf16[2,66,16,384]{3,2,1,0:T(8,128)(2,1)} %vis_hbm.1, s32[16,1536]{1,0:T(8,128)} %flag_hbm.1, bf16[1,384,1536]{2,1,0:T(8,128)(2,1)} %panel_ref.1), custom_call_target="tpu_custom_call" | custom-call | flops 4831838208 | bytes 6291456 | tf_op jit(solution)/shard_map/pallas_call | solution.py:390
  81.6 3.8 %copy.8 = bf16[2,1,32,16,1536]{4,3,2,1,0:T(8,128)(2,1)} copy(bf16[2,1,32,16,1536]{4,3,2,1,0:T(8,128)(2,1)} %shard_map.64) | data formatting | bytes 6291456

commit v6 on v4

--- a/solution.py
+++ b/solution.py
@@ -244,7 +244,6 @@
 
     near = my_z + 1 - 2 * lax.rem(my_z, 2)
     across = (z_peer(2), lax.rem(near + 2, groups))
-    inner = my_z % 3 != 0
 
     def send_all(q, carry):
         send_chunk(q, near)
@@ -259,10 +258,6 @@
     to_core.start()
     own_panel.start()
     lax.fori_loop(1, AHEAD, send_all, 0)
-
-    @pl.when(jnp.logical_not(inner))
-    def _():
-        lax.fori_loop(AHEAD, chunks, send_all, 0)
 
     for fetch in fetches[2:]:
         fetch.wait()
@@ -296,7 +291,7 @@
             x_copy(q, f_peer(d), my_f).start()
         land_x[q, my_f] = send_x[q, my_f]
 
-        @pl.when(jnp.logical_and(inner, q + AHEAD < chunks))
+        @pl.when(q + AHEAD < chunks)
         def _():
             send_all(q + AHEAD, 0)
 
@@ -338,7 +333,8 @@
     def filter_chunks(first, last):
         lax.fori_loop(first, last, filter_chunk, 0)
 
-    late = chunks - chunks // GROUP - 2
+    full_groups = chunks // GROUP - 1
+    late = chunks - full_groups - 3
     filter_chunks(0, 1)
     own_panel.wait()
     turn(my_f)
@@ -360,16 +356,14 @@
         filter_chunk(late + 2 + g, 0)
         return carry
 
-    full_groups = chunks // GROUP - 1
-    lax.fori_loop(0, full_groups, fit_group, 0)
-    fit_chunks(full_groups * GROUP, GROUP // 2)
-    filter_chunks(late + 2 + full_groups, chunks)
-
     def fit_one(q, carry):
         fit_chunks(q, 1)
         return carry
 
-    lax.fori_loop(full_groups * GROUP + GROUP // 2, chunks, fit_one, 0)
+    lax.fori_loop(0, full_groups, fit_group, 0)
+    fit_chunks(full_groups * GROUP, 2)
+    filter_chunks(chunks - 1, chunks)
+    lax.fori_loop(full_groups * GROUP + 2, chunks, fit_one, 0)
 
     def finish(q, carry):
         out_copy(q).wait()

time: 87.8 us -> 88.5 us (level)
  no operation moved by 1% of the time
where the time goes in v6:
time: 88.5 us; the launch traced here: 88.3 us
  Pallas kernels  84.6 us (96%)
  local copies, waits for them, and re-layouts  3.76 us (4%)
    pallas_call x1, Pallas kernels, kernel_shards(): pl.pallas_call(functools.partial(kernel, groups, lanes), out_shape=jax.Sh...  84.6 us
    unnamed x1, local copies, waits for them, and re-layouts  3.76 us

profile of v6, /device:TPU:0, one launch (start us, length us, event | category | flops | bytes accessed | tf_op | source)
XLA Modules:
  0.0 88.3 jit_solution(8269902651844700255)
XLA Ops:
  0.0 84.6 %shard_map.64 = bf16[2,1,32,16,1536]{4,3,2,1,0:T(8,128)(2,1)} custom-call(s32[4]{0:T(128)} %counts_hbm.1, s32[4]{0:T(128)} %windows_hbm.1, f32[2,4,9]{2,1,0:T(4,128)} %taps_hbm.1, bf16[2,66,16,384]{3,2,1,0:T(8,128)(2,1)} %vis_hbm.1, s32[16,1536]{1,0:T(8,128)} %flag_hbm.1, bf16[1,384,1536]{2,1,0:T(8,128)(2,1)} %panel_ref.1), custom_call_target="tpu_custom_call" | custom-call | flops 4831838208 | bytes 6291456 | tf_op jit(solution)/shard_map/pallas_call | solution.py:392
  84.6 3.8 %copy.8 = bf16[2,1,32,16,1536]{4,3,2,1,0:T(8,128)(2,1)} copy(bf16[2,1,32,16,1536]{4,3,2,1,0:T(8,128)(2,1)} %shard_map.64) | data formatting | bytes 6291456

commit v7 on v5

--- a/solution.py
+++ b/solution.py
@@ -9,9 +9,9 @@
 
 SLOTS = 32
 REACH = 4
-CHUNK = 4
-GROUP = 2
-AHEAD = 3
+SIZES = (8, 8, 4, 4, 4, 2, 2)
+STARTS = tuple(sum(SIZES[:k]) for k in range(len(SIZES)))
+AHEAD = 16
 MESH = pl.DeviceIdType.MESH
 
 
@@ -150,11 +150,9 @@
 ):
     my_z = lax.axis_index("tm")
     my_f = lax.axis_index("freq")
-    chunks = SLOTS // CHUNK
     block = vis_ref.shape[2]
     width = vis_ref.shape[3]
     baselines = vis_ref.shape[1]
-    rows = 2 * CHUNK * block
 
     def z_peer(d):
         return lax.rem(my_z + d, groups)
@@ -202,25 +200,36 @@
     to_core = panel_copy(1, panel_ref.at[0], my_f, core_peer)
     own_panel = pltpu.make_async_copy(panel_ref.at[0], panels.at[my_f], local_sem)
 
-    def z_copy(q, target, source):
+    def span(k):
+        return pl.ds(STARTS[k], SIZES[k])
+
+    def z_copy(k, target, source):
         return pltpu.make_async_remote_copy(
-            src_ref=send_z.at[q, target],
-            dst_ref=land_z.at[q, source],
-            send_sem=z_send_sem.at[q, target],
-            recv_sem=z_recv_sem.at[q, source],
+            src_ref=send_z.at[target, :, span(k)],
+            dst_ref=land_z.at[source, :, span(k)],
+            send_sem=z_send_sem.at[k, target],
+            recv_sem=z_recv_sem.at[k, source],
             device_id={"tm": target},
             device_id_type=MESH,
         )
 
-    def x_copy(q, target, source):
+    def x_copy(k, target, source):
         return pltpu.make_async_remote_copy(
-            src_ref=send_x.at[q, target],
-            dst_ref=land_x.at[q, source],
-            send_sem=x_send_sem.at[q, target],
-            recv_sem=x_recv_sem.at[q, source],
+            src_ref=send_x.at[target, :, span(k)],
+            dst_ref=land_x.at[source, :, span(k)],
+            send_sem=x_send_sem.at[k, target],
+            recv_sem=x_recv_sem.at[k, source],
             device_id={"freq": target},
             device_id_type=MESH,
         )
+
+    def pairs(first, count, body):
+        def pair(i, carry):
+            for u in range(2):
+                body(first + 2 * i + u)
+            return carry
+
+        lax.fori_loop(0, count // 2, pair, 0)
 
     def start_of(number):
         total = 0
@@ -228,48 +237,42 @@
             total = total + jnp.where(i < number, counts_ref[i], 0)
         return total
 
-    def pick(number, q, store):
-        first = start_of(number)
-        for s in range(CHUNK):
-            row = jnp.minimum(first + q * CHUNK + s, baselines - 1)
+    def pick(number, first, count, target_ref, place):
+        class_start = start_of(number)
+
+        def one(slot):
+            row = jnp.minimum(class_start + slot, baselines - 1)
             for r in range(2):
-                store(r, s, vis_ref[r, row])
-
-    def send_chunk(q, target):
-        def store(r, s, value):
-            send_z[q, target, r, s] = value
-
-        pick(target, q, store)
-        z_copy(q, target, my_z).start()
+                target_ref[place, r, slot] = vis_ref[r, row]
+
+        pairs(first, count, one)
+
+    def send_chunk(k, target):
+        pick(target, STARTS[k], SIZES[k], send_z, target)
+        z_copy(k, target, my_z).start()
 
     near = my_z + 1 - 2 * lax.rem(my_z, 2)
     across = (z_peer(2), lax.rem(near + 2, groups))
 
-    def send_all(q, carry):
-        send_chunk(q, near)
+    def send_all(k):
+        send_chunk(k, near)
         for target in across:
-            send_chunk(q, target)
-        return carry
+            send_chunk(k, target)
 
     fetches[0].wait()
     fetches[1].wait()
-    send_all(0, 0)
+    send_all(0)
     to_x.start()
     to_core.start()
     own_panel.start()
-    lax.fori_loop(1, AHEAD, send_all, 0)
+    sent = [k for k in range(len(SIZES)) if STARTS[k] < AHEAD]
+    for k in sent[1:]:
+        send_all(k)
 
     for fetch in fetches[2:]:
         fetch.wait()
 
-    def keep_chunk(q, carry):
-        def store(r, s, value):
-            land_z[q, my_z, r, s] = value
-
-        pick(my_z, q, store)
-        return carry
-
-    lax.fori_loop(0, chunks, keep_chunk, 0)
+    pick(my_z, 0, SLOTS, land_z, my_z)
 
     full = tap_matrix(taps_ref, windows_ref, my_z, groups * block, block)
     size = 2 * groups * block
@@ -278,100 +281,85 @@
     taps_mat[size:, :] = (full - high.astype(jnp.float32)).astype(jnp.bfloat16)
     live_count = counts_ref[my_z]
 
-    def filter_chunk(q, carry):
+    def filter_chunk(k):
         for d in range(1, groups):
-            z_copy(q, my_z, z_peer(d)).wait_recv()
-        for s in range(CHUNK):
-            cells = land_z[q, :, :, s].reshape(size, width)
+            z_copy(k, my_z, z_peer(d)).wait_recv()
+
+        def one(slot):
+            cells = land_z[:, :, slot].reshape(size, width)
             both = jnp.dot(taps_mat[...], cells, preferred_element_type=jnp.float32)
-            live = jnp.where(q * CHUNK + s < live_count, 1.0, 0.0)
+            live = jnp.where(slot < live_count, 1.0, 0.0)
             filtered = (both[:size] + both[size:]) * live
-            send_x[q, :, :, s] = filtered.astype(jnp.bfloat16).reshape(lanes, 2, block, width)
+            send_x[:, :, slot] = filtered.astype(jnp.bfloat16).reshape(lanes, 2, block, width)
+
+        pairs(STARTS[k], SIZES[k], one)
         for d in (2, 1, 3):
-            x_copy(q, f_peer(d), my_f).start()
-        land_x[q, my_f] = send_x[q, my_f]
-
-        @pl.when(q + AHEAD < chunks)
-        def _():
-            send_all(q + AHEAD, 0)
-
-        return carry
-
-    def out_copy(q):
+            x_copy(k, f_peer(d), my_f).start()
+        land_x[my_f, :, span(k)] = send_x[my_f, :, span(k)]
+        for later in range(len(SIZES)):
+            if later not in sent and STARTS[later] < STARTS[k] + SIZES[k] + AHEAD:
+                send_all(later)
+                sent.append(later)
+
+    def out_copy(k):
         return pltpu.make_async_copy(
-            result.at[q], out_ref.at[:, 0, pl.ds(q * CHUNK, CHUNK)], out_sem.at[q]
-        )
-
-    def fit_chunks(first, count):
-        for h in range(count):
-            for d in range(1, lanes):
-                x_copy(first + h, my_f, f_peer(d)).wait_recv()
-            for j in range(lanes):
-                gate = flag_ref[:, j * width : (j + 1) * width].astype(jnp.bfloat16)
-                weighted[h * rows : (h + 1) * rows, j * width : (j + 1) * width] = (
-                    land_x[first + h, j] * gate
-                ).reshape(rows, width)
+            result.at[:, span(k)], out_ref.at[:, 0, span(k)], out_sem.at[k]
+        )
+
+    def fit_chunk(k):
+        count = SIZES[k]
+        rows = 2 * count * block
+        for d in range(1, lanes):
+            x_copy(k, my_f, f_peer(d)).wait_recv()
+        for j in range(lanes):
+            gate = flag_ref[:, j * width : (j + 1) * width].astype(jnp.bfloat16)
+            weighted[:rows, j * width : (j + 1) * width] = (
+                land_x[j, :, span(k)] * gate
+            ).reshape(rows, width)
 
         def one_block(i, carry):
-            fit = jnp.dot(
-                weighted[: count * rows], panels_t[i], preferred_element_type=jnp.float32
-            )
+            fit = jnp.dot(weighted[:rows], panels_t[i], preferred_element_type=jnp.float32)
             columns = pl.ds(pl.multiple_of(i * width, width), width)
-            for h in range(count):
-                slotted = land_x[first + h, i].astype(jnp.float32).reshape(rows, width)
-                cleaned = (slotted - fit[h * rows : (h + 1) * rows]).astype(jnp.bfloat16)
-                result[first + h, :, :, :, columns] = cleaned.reshape(2, CHUNK, block, width)
+            slotted = land_x[i, :, span(k)].astype(jnp.float32).reshape(rows, width)
+            cleaned = (slotted - fit).astype(jnp.bfloat16)
+            result[:, span(k), :, columns] = cleaned.reshape(2, count, block, width)
             return carry
 
         lax.fori_loop(0, lanes, one_block, 0)
-        for h in range(count):
-            out_copy(first + h).start()
+        out_copy(k).start()
 
     def turn(i):
         panels_t[i] = panels[i].T
 
-    def filter_chunks(first, last):
-        lax.fori_loop(first, last, filter_chunk, 0)
-
-    half = chunks // 2
-    filter_chunks(0, 1)
     own_panel.wait()
     turn(my_f)
-    filter_chunks(1, 2)
+    filter_chunk(0)
     panel_copy(1, panel_ref.at[0], core_peer, my_f).wait_recv()
     turn(core_peer)
-    filter_chunks(2, half + 1)
+    filter_chunk(1)
     panel_copy(0, panel_ref.at[0], x_peer, my_f).wait_recv()
     forward = panel_copy(2, panels.at[x_peer], x_peer, core_peer)
     forward.start()
     turn(x_peer)
-    filter_chunks(half + 1, half + 2)
+    filter_chunk(2)
     panel_copy(2, panel_ref.at[0], far_peer, my_f).wait_recv()
     turn(far_peer)
-
-    def fit_group(g, carry):
-        fit_chunks(g * GROUP, GROUP)
-        return carry
-
-    def fit_one(q, carry):
-        fit_chunks(q, 1)
-        return carry
-
-    lax.fori_loop(0, 1, fit_group, 0)
-    filter_chunks(half + 2, chunks - 1)
-    lax.fori_loop(1, chunks // GROUP - 1, fit_group, 0)
-    filter_chunks(chunks - 1, chunks)
-    lax.fori_loop(chunks - GROUP, chunks, fit_one, 0)
-
-    def finish(q, carry):
-        out_copy(q).wait()
+    last = len(SIZES) - 1
+    fit_chunk(0)
+    for k in range(3, last):
+        filter_chunk(k)
+        fit_chunk(k - 2)
+    fit_chunk(last - 2)
+    filter_chunk(last)
+    fit_chunk(last - 1)
+    fit_chunk(last)
+
+    for k in range(len(SIZES)):
+        out_copy(k).wait()
         for d in range(1, groups):
-            z_copy(q, z_peer(d), my_z).wait_send()
+            z_copy(k, z_peer(d), my_z).wait_send()
         for d in range(1, lanes):
-            x_copy(q, f_peer(d), my_f).wait_send()
-        return carry
-
-    lax.fori_loop(0, chunks, finish, 0)
+            x_copy(k, f_peer(d), my_f).wait_send()
     to_x.wait_send()
     to_core.wait_send()
     forward.wait_send()
@@ -382,7 +370,7 @@
 ):
     block, width = visibilities.shape[2:]
     channels = lanes * width
-    chunks = SLOTS // CHUNK
+    chunks = len(SIZES)
     size = 2 * groups * block
     bf16 = jnp.bfloat16
     hbm = pl.BlockSpec(memory_space=pltpu.HBM)
@@ -398,15 +386,15 @@
             pltpu.SMEM(fringe_taps.shape, jnp.float32),
             pltpu.VMEM(flag_mask.shape, jnp.int32),
             pltpu.VMEM(visibilities.shape, bf16),
-            pltpu.VMEM((chunks, groups, 2, CHUNK, block, width), bf16),
-            pltpu.VMEM((chunks, groups, 2, CHUNK, block, width), bf16),
-            pltpu.VMEM((chunks, lanes, 2, CHUNK, block, width), bf16),
-            pltpu.VMEM((chunks, lanes, 2, CHUNK, block, width), bf16),
+            pltpu.VMEM((groups, 2, SLOTS, block, width), bf16),
+            pltpu.VMEM((groups, 2, SLOTS, block, width), bf16),
+            pltpu.VMEM((lanes, 2, SLOTS, block, width), bf16),
+            pltpu.VMEM((lanes, 2, SLOTS, block, width), bf16),
             pltpu.VMEM((lanes, width, channels), bf16),
             pltpu.VMEM((lanes, channels, width), bf16),
             pltpu.VMEM((2 * size, size), bf16),
-            pltpu.VMEM((GROUP * 2 * CHUNK * block, channels), bf16),
-            pltpu.VMEM((chunks, 2, CHUNK, block, channels), bf16),
+            pltpu.VMEM((2 * max(SIZES) * block, channels), bf16),
+            pltpu.VMEM((2, SLOTS, block, channels), bf16),
             dma((chunks, groups)),
             dma((chunks, groups)),
             dma((chunks, lanes)),

time: 86.1 us -> 88.9 us (1.033)
  Pallas kernels: 81.6 us -> 83.5 us
    pallas_call x1, Pallas kernels: 81.6 us -> 83.5 us  [kernel_shards(): pl.pallas_call(functools.partial(kernel, groups, lanes), out_shape=jax.Sh...]
where the time goes in v7:
time: 88.9 us; the launch traced here: 87.3 us
  Pallas kernels  83.5 us (94%)
  local copies, waits for them, and re-layouts  3.76 us (4%)
    pallas_call x1, Pallas kernels, kernel_shards(): pl.pallas_call(functools.partial(kernel, groups, lanes), out_shape=jax.Sh...  83.5 us
    unnamed x1, local copies, waits for them, and re-layouts  3.76 us

profile of v7, /device:TPU:0, one launch (start us, length us, event | category | flops | bytes accessed | tf_op | source)
XLA Modules:
  0.0 87.3 jit_solution(3459488480766727503)
XLA Ops:
  0.0 83.5 %shard_map.64 = bf16[2,1,32,16,1536]{4,3,2,1,0:T(8,128)(2,1)} custom-call(s32[4]{0:T(128)} %counts_hbm.1, s32[4]{0:T(128)} %windows_hbm.1, f32[2,4,9]{2,1,0:T(4,128)} %taps_hbm.1, bf16[2,66,16,384]{3,2,1,0:T(8,128)(2,1)} %vis_hbm.1, s32[16,1536]{1,0:T(8,128)} %flag_hbm.1, bf16[1,384,1536]{2,1,0:T(8,128)(2,1)} %panel_ref.1), custom_call_target="tpu_custom_call" | custom-call | flops 4831838208 | bytes 6291456 | tf_op jit(solution)/shard_map/pallas_call | solution.py:378
  83.5 3.8 %copy.8 = bf16[2,1,32,16,1536]{4,3,2,1,0:T(8,128)(2,1)} copy(bf16[2,1,32,16,1536]{4,3,2,1,0:T(8,128)(2,1)} %shard_map.64) | data formatting | bytes 6291456

commit v8 on v7

--- a/solution.py
+++ b/solution.py
@@ -9,7 +9,7 @@
 
 SLOTS = 32
 REACH = 4
-SIZES = (8, 8, 4, 4, 4, 2, 2)
+SIZES = (8, 8, 8, 4, 4)
 STARTS = tuple(sum(SIZES[:k]) for k in range(len(SIZES)))
 AHEAD = 16
 MESH = pl.DeviceIdType.MESH
@@ -90,13 +90,13 @@
     return (local_block.astype(jnp.float32) - dayenu_fit).astype(jnp.bfloat16)
 
 
-def tap_matrix(taps_ref, windows_ref, own_class, steps, block):
+def tap_matrix(taps_ref, windows_ref, own_class, steps):
     size = 2 * steps
     out_pos = lax.broadcasted_iota(jnp.int32, (size, size), 0)
     in_pos = lax.broadcasted_iota(jnp.int32, (size, size), 1)
 
     def parts(pos):
-        return (pos // (2 * block)) * block + pos % block, (pos // block) % 2
+        return pos % steps, pos // steps
 
     out_t, out_r = parts(out_pos)
     in_t, in_r = parts(in_pos)
@@ -203,10 +203,16 @@
     def span(k):
         return pl.ds(STARTS[k], SIZES[k])
 
+    def both_spans(k):
+        return pl.ds(2 * STARTS[k], 2 * SIZES[k])
+
+    def place_of(k, r, slot):
+        return STARTS[k] + r * SIZES[k] + slot
+
     def z_copy(k, target, source):
         return pltpu.make_async_remote_copy(
-            src_ref=send_z.at[target, :, span(k)],
-            dst_ref=land_z.at[source, :, span(k)],
+            src_ref=send_z.at[target, both_spans(k)],
+            dst_ref=land_z.at[source, both_spans(k)],
             send_sem=z_send_sem.at[k, target],
             recv_sem=z_recv_sem.at[k, source],
             device_id={"tm": target},
@@ -215,8 +221,8 @@
 
     def x_copy(k, target, source):
         return pltpu.make_async_remote_copy(
-            src_ref=send_x.at[target, :, span(k)],
-            dst_ref=land_x.at[source, :, span(k)],
+            src_ref=send_x.at[target, both_spans(k)],
+            dst_ref=land_x.at[source, both_spans(k)],
             send_sem=x_send_sem.at[k, target],
             recv_sem=x_recv_sem.at[k, source],
             device_id={"freq": target},
@@ -237,18 +243,18 @@
             total = total + jnp.where(i < number, counts_ref[i], 0)
         return total
 
-    def pick(number, first, count, target_ref, place):
+    def pick(number, k, target_ref):
         class_start = start_of(number)
 
         def one(slot):
             row = jnp.minimum(class_start + slot, baselines - 1)
             for r in range(2):
-                target_ref[place, r, slot] = vis_ref[r, row]
-
-        pairs(first, count, one)
+                target_ref[number, place_of(k, r, slot)] = vis_ref[r, row]
+
+        pairs(STARTS[k], SIZES[k], one)
 
     def send_chunk(k, target):
-        pick(target, STARTS[k], SIZES[k], send_z, target)
+        pick(target, k, send_z)
         z_copy(k, target, my_z).start()
 
     near = my_z + 1 - 2 * lax.rem(my_z, 2)
@@ -272,10 +278,12 @@
     for fetch in fetches[2:]:
         fetch.wait()
 
-    pick(my_z, 0, SLOTS, land_z, my_z)
-
-    full = tap_matrix(taps_ref, windows_ref, my_z, groups * block, block)
-    size = 2 * groups * block
+    for k in range(len(SIZES)):
+        pick(my_z, k, land_z)
+
+    steps = groups * block
+    full = tap_matrix(taps_ref, windows_ref, my_z, steps)
+    size = 2 * steps
     high = full.astype(jnp.bfloat16)
     taps_mat[:size, :] = high
     taps_mat[size:, :] = (full - high.astype(jnp.float32)).astype(jnp.bfloat16)
@@ -286,16 +294,21 @@
             z_copy(k, my_z, z_peer(d)).wait_recv()
 
         def one(slot):
-            cells = land_z[:, :, slot].reshape(size, width)
+            cells = jnp.concatenate(
+                [land_z[:, place_of(k, r, slot)].reshape(steps, width) for r in range(2)]
+            )
             both = jnp.dot(taps_mat[...], cells, preferred_element_type=jnp.float32)
             live = jnp.where(slot < live_count, 1.0, 0.0)
             filtered = (both[:size] + both[size:]) * live
-            send_x[:, :, slot] = filtered.astype(jnp.bfloat16).reshape(lanes, 2, block, width)
+            filtered = filtered.astype(jnp.bfloat16)
+            for r in range(2):
+                part = filtered[r * steps : (r + 1) * steps]
+                send_x[:, place_of(k, r, slot)] = part.reshape(lanes, block, width)
 
         pairs(STARTS[k], SIZES[k], one)
         for d in (2, 1, 3):
             x_copy(k, f_peer(d), my_f).start()
-        land_x[my_f, :, span(k)] = send_x[my_f, :, span(k)]
+        land_x[my_f, both_spans(k)] = send_x[my_f, both_spans(k)]
         for later in range(len(SIZES)):
             if later not in sent and STARTS[later] < STARTS[k] + SIZES[k] + AHEAD:
                 send_all(later)
@@ -314,13 +327,13 @@
         for j in range(lanes):
             gate = flag_ref[:, j * width : (j + 1) * width].astype(jnp.bfloat16)
             weighted[:rows, j * width : (j + 1) * width] = (
-                land_x[j, :, span(k)] * gate
+                land_x[j, both_spans(k)] * gate
             ).reshape(rows, width)
 
         def one_block(i, carry):
             fit = jnp.dot(weighted[:rows], panels_t[i], preferred_element_type=jnp.float32)
             columns = pl.ds(pl.multiple_of(i * width, width), width)
-            slotted = land_x[i, :, span(k)].astype(jnp.float32).reshape(rows, width)
+            slotted = land_x[i, both_spans(k)].astype(jnp.float32).reshape(rows, width)
             cleaned = (slotted - fit).astype(jnp.bfloat16)
             result[:, span(k), :, columns] = cleaned.reshape(2, count, block, width)
             return carry
@@ -386,10 +399,10 @@
             pltpu.SMEM(fringe_taps.shape, jnp.float32),
             pltpu.VMEM(flag_mask.shape, jnp.int32),
             pltpu.VMEM(visibilities.shape, bf16),
-            pltpu.VMEM((groups, 2, SLOTS, block, width), bf16),
-            pltpu.VMEM((groups, 2, SLOTS, block, width), bf16),
-            pltpu.VMEM((lanes, 2, SLOTS, block, width), bf16),
-            pltpu.VMEM((lanes, 2, SLOTS, block, width), bf16),
+            pltpu.VMEM((groups, 2 * SLOTS, block, width), bf16),
+            pltpu.VMEM((groups, 2 * SLOTS, block, width), bf16),
+            pltpu.VMEM((lanes, 2 * SLOTS, block, width), bf16),
+            pltpu.VMEM((lanes, 2 * SLOTS, block, width), bf16),
             pltpu.VMEM((lanes, width, channels), bf16),
             pltpu.VMEM((lanes, channels, width), bf16),
             pltpu.VMEM((2 * size, size), bf16),

time: 88.9 us -> 90.1 us (1.013)
  Pallas kernels: 83.5 us -> 84.7 us
    pallas_call x1, Pallas kernels: 83.5 us -> 84.7 us  [kernel_shards(): pl.pallas_call(functools.partial(kernel, groups, lanes), out_shape=jax.Sh...]
where the time goes in v8:
time: 90.1 us; the launch traced here: 88.4 us
  Pallas kernels  84.7 us (94%)
  local copies, waits for them, and re-layouts  3.76 us (4%)
    pallas_call x1, Pallas kernels, kernel_shards(): pl.pallas_call(functools.partial(kernel, groups, lanes), out_shape=jax.Sh...  84.7 us
    unnamed x1, local copies, waits for them, and re-layouts  3.76 us

profile of v8, /device:TPU:0, one launch (start us, length us, event | category | flops | bytes accessed | tf_op | source)
XLA Modules:
  0.0 88.4 jit_solution(15309510318670404611)
XLA Ops:
  0.0 84.7 %shard_map.64 = bf16[2,1,32,16,1536]{4,3,2,1,0:T(8,128)(2,1)} custom-call(s32[4]{0:T(128)} %counts_hbm.1, s32[4]{0:T(128)} %windows_hbm.1, f32[2,4,9]{2,1,0:T(4,128)} %taps_hbm.1, bf16[2,66,16,384]{3,2,1,0:T(8,128)(2,1)} %vis_hbm.1, s32[16,1536]{1,0:T(8,128)} %flag_hbm.1, bf16[1,384,1536]{2,1,0:T(8,128)(2,1)} %panel_ref.1), custom_call_target="tpu_custom_call" | custom-call | flops 4831838208 | bytes 6291456 | tf_op jit(solution)/shard_map/pallas_call | solution.py:391
  84.7 3.8 %copy.8 = bf16[2,1,32,16,1536]{4,3,2,1,0:T(8,128)(2,1)} copy(bf16[2,1,32,16,1536]{4,3,2,1,0:T(8,128)(2,1)} %shard_map.64) | data formatting | bytes 6291456
